TPU v7x, 32 devices: a whole 2x2x4 slice. The times are simulated.
32 devices in a mesh: lat: 4 (over z), lon: 4 (over y, core), buf: 2 (over x).
Axes of the slice: x: 2, y: 2, z: 4, core: 2. Of those that a mesh axis runs over, the one named last changes fastest.
Arguments:
- store: bfloat16 [8, 64, 64, 1725], P('buf', ('lat', 'lon')), may hold values from -6 to 6
- sample_index: int32 [6], replicated, may hold values from 0 to 7, as said below
- region_ids: int32 [64, 64], replicated, may hold values from 0 to 2
- w_embed: bfloat16 [1725, 512], replicated, may hold values from -0.15625 to 0.15625
- attn_gain: float32 [512], replicated, may hold values from 0.1 to 1.9
- w_qkv: bfloat16 [512, 1536], replicated, may hold values from -8 to 8
- w_out: bfloat16 [512, 512], replicated, may hold values from -0.25 to 0.25
- out_gain: float32 [512], replicated, may hold values from 0.1 to 1.9
- w_dec: bfloat16 [512, 1725], replicated, may hold values from -0.25 to 0.25
Outputs:
- new_store: bfloat16 [8, 64, 64, 1725], P('buf', ('lat', 'lon'))
Inputs may be any that keep to these rules, and one draw needn't show every extreme that they name: `sample_index`: distinct slot numbers.
All inputs are finite; a program needn't handle non-finite values.
Results may differ from a plain program's by a relative error of at most 0.007.
Values may be sent and summed in bfloat16 or wider, within the bound.
A program may use at most 128 MiB of HBM per device.

v0:
```python
import math
import jax
import jax.numpy as jnp
from jax import lax
from jax.sharding import PartitionSpec as P

D = 512
HEADS = 8
HDIM = 64
WIN = 8


def with_halo(array, sides, width):
    for axis, dim in sides:
        devices, length = (lax.axis_size(axis), array.shape[dim])
        up = [(i, (i + 1) % devices) for i in range(devices)]
        down = [(j, i) for i, j in up]
        last = lax.slice_in_dim(array, length - width, length, axis=dim)
        leading = lax.slice_in_dim(array, 0, width, axis=dim)
        before = lax.ppermute(last, axis, up)
        after = lax.ppermute(leading, axis, down)
        array = jnp.concatenate([before, array, after], axis=dim)
    return array


def layer_norm(values, gain_row):
    center = jnp.mean(values, axis=-1, keepdims=True)
    spread = jnp.mean(jnp.square(values - center), axis=-1, keepdims=True)
    return (values - center) * lax.rsqrt(spread + 1e-05) * gain_row


def window_mix(windows, regions):
    scores = jnp.einsum(
        "bwqhd,bwkhd->bwhqk",
        windows[:, :, :, 0],
        windows[:, :, :, 1],
        preferred_element_type=jnp.float32,
    ) / math.sqrt(HDIM)
    visible = (regions[:, :, None] == regions[:, None, :])[None, :, None]
    scores = jnp.where(visible, scores, -1e30)
    highest = jnp.max(scores, axis=-1, keepdims=True)
    expo_terms = jnp.where(visible, jnp.exp(scores - highest), 0.0)
    weights = (expo_terms / jnp.sum(expo_terms, axis=-1, keepdims=True)).astype(jnp.bfloat16)
    return jnp.einsum(
        "bwhqk,bwkhd->bwqhd", weights, windows[:, :, :, 2], preferred_element_type=jnp.float32
    ).astype(jnp.bfloat16)


def local(store, sample_index, region_ids, w_embed, attn_gain, w_qkv, w_out, out_gain, w_dec):
    lon_count = lax.axis_size("lon")
    slots_here, rows_here, width_all, patch_len = store.shape
    patch_cols = width_all // lon_count
    patch_rows = rows_here * lon_count
    half_win = WIN // 2
    ext_rows = patch_rows + WIN
    ext_cols = patch_cols + WIN
    own_slots = lax.axis_index("buf") * slots_here + jnp.arange(slots_here, dtype=jnp.int32)
    matches = own_slots[:, None] == sample_index[None, :]
    occupied = jnp.any(matches, axis=1)
    local_rows = store.reshape(slots_here, 1, rows_here, lon_count, patch_cols, patch_len)
    tile_data = lax.all_to_all(local_rows, "lon", split_axis=3, concat_axis=1, tiled=True)
    patches = tile_data.reshape(-1, patch_len)
    embedded = jnp.dot(patches, w_embed, preferred_element_type=jnp.float32).astype(jnp.bfloat16)
    normed = layer_norm(embedded.astype(jnp.float32), attn_gain).astype(jnp.bfloat16)
    normed = normed.reshape(slots_here, patch_rows, patch_cols, D)
    widened = with_halo(normed, (("lat", 1), ("lon", 2)), half_win)
    projected = jnp.dot(widened.reshape(-1, D), w_qkv, preferred_element_type=jnp.float32).astype(
        jnp.bfloat16
    )
    windows = projected.reshape(
        slots_here, ext_rows // WIN, WIN, ext_cols // WIN, WIN, 3, HEADS, HDIM
    )
    windows = windows.transpose(0, 1, 3, 2, 4, 5, 6, 7).reshape(
        slots_here, -1, WIN * WIN, 3, HEADS, HDIM
    )
    total_rows, total_cols = region_ids.shape
    row_pick = (
        lax.axis_index("lat") * patch_rows - half_win + jnp.arange(ext_rows, dtype=jnp.int32)
    ) % total_rows
    col_pick = (
        lax.axis_index("lon") * patch_cols - half_win + jnp.arange(ext_cols, dtype=jnp.int32)
    ) % total_cols
    local_regions = jnp.take(jnp.take(region_ids, row_pick, axis=0), col_pick, axis=1)
    region_windows = (
        local_regions.reshape(ext_rows // WIN, WIN, ext_cols // WIN, WIN)
        .transpose(0, 2, 1, 3)
        .reshape(-1, WIN * WIN)
    )
    mixed_heads = window_mix(windows, region_windows)
    placed = mixed_heads.reshape(slots_here, ext_rows // WIN, ext_cols // WIN, WIN, WIN, D)
    placed = placed.transpose(0, 1, 3, 2, 4, 5).reshape(slots_here, ext_rows, ext_cols, D)
    placed = placed[:, half_win : half_win + patch_rows, half_win : half_win + patch_cols].reshape(
        -1, D
    )
    updated = embedded.astype(jnp.float32) + jnp.dot(
        placed, w_out, preferred_element_type=jnp.float32
    )
    final_norm = layer_norm(updated, out_gain).astype(jnp.bfloat16)
    predicted = (
        patches.astype(jnp.float32) + jnp.dot(final_norm, w_dec, preferred_element_type=jnp.float32)
    ).astype(jnp.bfloat16)
    outgoing = predicted.reshape(slots_here, lon_count, rows_here, 1, patch_cols, patch_len)
    returned = lax.all_to_all(outgoing, "lon", split_axis=1, concat_axis=3, tiled=True)
    strip_data = returned.reshape(slots_here, rows_here, width_all, patch_len)
    return jnp.where(occupied[:, None, None, None], strip_data, store)


def solution(mesh):
    return jax.shard_map(
        local,
        mesh=mesh,
        in_specs=(P("buf", ("lat", "lon"), None, None), P(), P(), P(), P(), P(), P(), P(), P()),
        out_specs=P("buf", ("lat", "lon"), None, None),
        check_vma=False,
    )
```

profile of v0, /device:TPU:0, one launch (start us, length us, event | category | flops | bytes accessed | tf_op | source)
XLA Modules:
  0.0 231.9 jit_solution(15052900297631613152)
XLA Ops:
  0.0 4.4 %copy.71 = bf16[4,1,4,4,16,1725]{5,4,2,0,1,3:T(8,128)(2,1)} copy(bf16[4,1,4,4,16,1725]{5,4,3,2,0,1:T(8,128)(2,1)} %bitcast.55) | data formatting | bytes 7065600 | tf_op jit(solution)/shard_map/reshape | solution.py:60
  4.4 4.9 %all-to-all-start = ((bf16[4,1,4,4,16,1725]{5,4,2,0,1,3:T(8,128)(2,1)}), bf16[4,1,4,4,16,1725]{5,4,2,0,1,3:T(8,128)(2,1)}, u32[]{:S(2)}, u32[]{:S(2)}) async-start(bf16[4,1,4,4,16,1725]{5,4,2,0,1,3:T(8,128)(2,1)} %copy.71), calls=%async_computation | async-start | bytes 7340032 | tf_op jit(solution)/shard_map/all_to_all | solution.py:61
  10.0 42.5 %all-to-all-done = bf16[4,1,4,4,16,1725]{5,4,2,0,1,3:T(8,128)(2,1)} async-done(((bf16[4,1,4,4,16,1725]{5,4,2,0,1,3:T(8,128)(2,1)}), bf16[4,1,4,4,16,1725]{5,4,2,0,1,3:T(8,128)(2,1)}, u32[]{:S(2)}, u32[]{:S(2)}) %all-to-all-start) | async-done | bytes 3532832 | tf_op jit(solution)/shard_map/all_to_all | solution.py:61
  52.6 2.4 %copy.72 = bf16[4,4,1,4,1,16,1725]{6,5,3,1,0,4,2:T(8,128)(2,1)S(1)} copy(bf16[4,4,1,4,1,16,1725]{6,5,3,0,1,4,2:T(8,128)(2,1)} %bitcast.2) | data formatting | bytes 7065600 | tf_op jit(solution)/shard_map/all_to_all | solution.py:61
  55.1 2.1 convert_reduce_fusion
  58.7 0.8 fusion.24
  59.5 2.4 %collective-permute-start = (bf16[4,4,16,512]{3,2,1,0:T(8,128)(2,1)}, bf16[4,4,16,512]{3,2,1,0:T(8,128)(2,1)S(1)}, u32[]{:S(2)}, u32[]{:S(2)}) collective-permute-start(bf16[4,4,16,512]{3,2,1,0:T(8,128)(2,1)} %get-tuple-element.7), channel_id=1, source_target_pairs={{0,8},{8,16},{16,24},{24,0},{1,9},{9,17},{17,25},{25,1},{2,10},{10... | collective-permute-start | bytes 786440 | tf_op jit(solution)/shard_map/ppermute | solution.py:20
  61.9 2.0 collective-permute-start.1
  64.8 6.6 %collective-permute-done = bf16[4,4,16,512]{3,2,1,0:T(8,128)(2,1)S(1)} collective-permute-done((bf16[4,4,16,512]{3,2,1,0:T(8,128)(2,1)}, bf16[4,4,16,512]{3,2,1,0:T(8,128)(2,1)S(1)}, u32[]{:S(2)}, u32[]{:S(2)}) %collective-permute-start) | collective-permute-done | bytes 262176 | tf_op jit(solution)/shard_map/ppermute | solution.py:20
  71.4 3.9 %collective-permute-done.1 = bf16[4,4,16,512]{3,2,1,0:T(8,128)(2,1)S(1)} collective-permute-done((bf16[4,4,16,512]{3,2,1,0:T(8,128)(2,1)}, bf16[4,4,16,512]{3,2,1,0:T(8,128)(2,1)S(1)}, u32[]{:S(2)}, u32[]{:S(2)}) %collective-permute-start.1) | collective-permute-done | bytes 262176 | tf_op jit(solution)/shard_map/ppermute | solution.py:21
  75.3 1.2 pad_maximum_fusion.3
  76.5 1.7 collective-permute-start.3
  78.5 5.9 %copy.73 = bf16[1024,1725]{0,1:T(8,128)(2,1)} copy(bf16[1024,1725]{1,0:T(8,128)(2,1)} %bitcast.53) | data formatting | bytes 7065600 | tf_op jit(solution)/shard_map/reshape | solution.py:62
  84.5 2.9 %collective-permute-done.2 = bf16[4,24,4,512]{3,2,1,0:T(4,128)(2,1)} collective-permute-done((bf16[4,24,4,512]{3,2,1,0:T(4,128)(2,1)}, bf16[4,24,4,512]{3,2,1,0:T(4,128)(2,1)}, u32[]{:S(2)}, u32[]{:S(2)}) %collective-permute-start.2) | collective-permute-done | bytes 393248 | tf_op jit(solution)/shard_map/ppermute | solution.py:20
  87.4 2.8 %pad_maximum_fusion = bf16[4,24,24,512]{3,2,1,0:T(8,128)(2,1)S(1)} fusion(bf16[4,24,4,512]{3,2,1,0:T(4,128)(2,1)} %collective-permute-done.3, bf16[4,4,16,512]{3,2,1,0:T(8,128)(2,1)S(1)} %collective-permute-done.1, bf16[4,16,16,512]{3,2,1,0:T(8,128)(2,1)S(1)} %bitcast.59, bf16[4,4,16,512]{3,2,1,0:T(8,128)(2,1)S(1)} %collective-permute-done, ...), kind=kLoop, calls=%fused_computation.25 | loop fusion | flops 11796480 | bytes 4718592 | tf_op jit(solution)/shard_map/concatenate | solution.py:22
  90.2 5.8 %convolution_convert_fusion = bf16[2304,1536]{1,0:T(8,128)(2,1)} fusion(bf16[2304,512]{1,0:T(8,128)(2,1)S(1)} %bitcast.63, bf16[512,1536]{1,0:T(8,128)(2,1)S(1)} %copy-done.10), kind=kOutput, calls=%fused_computation.3 | convolution fusion | flops 3627417600 | bytes 11010048 | tf_op jit(solution)/shard_map/dot_general | solution.py:67
  96.0 18.0 %reshape.191 = bf16[4,3,8,3,8,3,8,64]{7,6,5,4,3,2,1,0:T(8,128)(2,1)} reshape(bf16[2304,1536]{1,0:T(8,128)(2,1)} %convolution_convert_fusion) | data formatting | bytes 14155776 | tf_op jit(solution)/shard_map/reshape | solution.py:70
  114.0 11.2 %copy.74 = bf16[4,3,3,8,8,3,8,64]{7,4,3,6,2,1,0,5:T(8,128)(2,1)} copy(bf16[4,3,3,8,8,3,8,64]{7,6,5,4,2,3,1,0:T(8,128)(2,1)} %bitcast.51) | data formatting | bytes 14155776 | tf_op jit(solution)/shard_map/transpose | solution.py:73
  125.2 6.4 %fusion.3 = f32[4,9,8,64,64]{3,4,2,1,0:T(8,128)S(1)} fusion(bf16[4,9,64,3,8,64]{5,2,4,1,0,3:T(8,128)(2,1)} %bitcast.49), kind=kOutput, calls=%fused_computation.11 | convolution fusion | flops 150994944 | bytes 14155776 | tf_op jit(solution)/shard_map/bwqhd,bwkhd->bwhqk/dot_general | solution.py:33
  131.6 5.4 %fusion.25 = (f32[4,9,8,64]{3,2,1,0:T(8,128)S(1)}, f32[4,9,8,64,64]{3,4,2,1,0:T(8,128)}) fusion(f32[4,9,8,64,64]{3,4,2,1,0:T(8,128)S(1)} %fusion.3, pred[9,64,64]{1,2,0:T(8,128)(4,1)S(1)} %broadcast_compare_fusion), kind=kOutput, calls=%fused_computation.76 | output fusion | flops 8257599 | bytes 9547776 | tf_op jit(solution)/shard_map/sub | solution.py:42
  137.0 9.2 %convert_bitcast_fusion = bf16[4,9,64,8,64]{2,4,3,1,0:T(8,128)(2,1)} fusion(f32[4,9,8,64,64]{3,4,2,1,0:T(8,128)} %get-tuple-element.12, f32[4,9,8,64]{3,2,1,0:T(8,128)S(1)} %get-tuple-element.11, bf16[4,9,64,3,8,64]{5,2,4,1,0,3:T(8,128)(2,1)} %bitcast.50), kind=kOutput, calls=%fused_computation.14 | convolution fusion | flops 154533888 | bytes 16588800 | tf_op jit(solution)/shard_map/bwhqk,bwkhd->bwqhd/dot_general | solution.py:44
  146.2 7.0 %copy.80 = bf16[4,9,64,8,64]{4,3,2,1,0:T(8,128)(2,1)} copy(bf16[4,9,64,8,64]{2,4,3,1,0:T(8,128)(2,1)} %convert_bitcast_fusion) | data formatting | bytes 4718592 | tf_op jit(solution)/shard_map/convert_element_type | solution.py:46
  153.1 7.4 %reshape.193 = bf16[4,3,3,8,8,512]{5,4,3,2,1,0:T(8,128)(2,1)} reshape(bf16[4,9,64,8,64]{4,3,2,1,0:T(8,128)(2,1)} %copy.80) | data formatting | bytes 4718592 | tf_op jit(solution)/shard_map/reshape | solution.py:90
  160.5 1.9 copy.81
  163.0 0.8 fusion.26
  164.9 4.1 %add_convert_fusion = bf16[1024,1725]{0,1:T(8,128)(2,1)} fusion(bf16[1024,1725]{0,1:T(8,128)(2,1)S(1)} %copy-done.5, bf16[512,1725]{0,1:T(8,128)(2,1)S(1)} %copy-done, f32[1024,512]{1,0:T(8,128)S(1)} %get-tuple-element.14, f32[512]{0:T(512)S(1)} %copy-done.11, f32[1024]{0:T(1024)S(1)} %add_rsqrt_fusion, f32[1024]{0:T(1024)S(1)} %broadcast_multiply_fusion), kind=kOutput, calls=%fused_computation.8 | convolution fusion | flops 1816189952 | bytes 10939392 | tf_op jit(solution)/shard_map/dot_general | solution.py:100
  169.0 5.8 %copy.83 = bf16[1024,1725]{1,0:T(8,128)(2,1)} copy(bf16[1024,1725]{0,1:T(8,128)(2,1)} %add_convert_fusion) | data formatting | bytes 7065600 | tf_op jit(solution)/shard_map/convert_element_type | solution.py:101
  174.8 4.2 %copy.84 = bf16[4,4,4,1,16,1725]{5,4,2,0,3,1:T(8,128)(2,1)} copy(bf16[4,4,4,1,16,1725]{5,4,2,1,0,3:T(8,128)(2,1)} %bitcast.54) | data formatting | bytes 7065600 | tf_op jit(solution)/shard_map/reshape | solution.py:102
  179.0 4.9 %all-to-all-start.1 = ((bf16[4,4,4,1,16,1725]{5,4,2,0,3,1:T(8,128)(2,1)}), bf16[4,4,4,1,16,1725]{5,4,2,0,3,1:T(8,128)(2,1)}, u32[]{:S(2)}, u32[]{:S(2)}) async-start(bf16[4,4,4,1,16,1725]{5,4,2,0,3,1:T(8,128)(2,1)} %copy.84), calls=%async_computation.1 | async-start | bytes 7340032 | tf_op jit(solution)/shard_map/all_to_all | solution.py:103
  184.1 42.4 %all-to-all-done.1 = bf16[4,4,4,1,16,1725]{5,4,2,0,3,1:T(8,128)(2,1)} async-done(((bf16[4,4,4,1,16,1725]{5,4,2,0,3,1:T(8,128)(2,1)}), bf16[4,4,4,1,16,1725]{5,4,2,0,3,1:T(8,128)(2,1)}, u32[]{:S(2)}, u32[]{:S(2)}) %all-to-all-start.1) | async-done | bytes 3532832 | tf_op jit(solution)/shard_map/all_to_all | solution.py:103
  226.5 2.6 %copy.85 = bf16[4,4,4,1,16,1725]{5,4,1,2,0,3:T(8,128)(2,1)S(1)} copy(bf16[4,4,4,1,16,1725]{5,4,2,0,3,1:T(8,128)(2,1)} %all-to-all-done.1) | data formatting | bytes 7065600 | tf_op jit(solution)/shard_map/all_to_all | solution.py:103
  229.7 2.3 broadcast_select_fusion
  (54 shorter events, 5.7 us)
Async XLA Ops:
  0.0 164.2 %copy-start = (bf16[512,1725]{0,1:T(8,128)(2,1)S(1)}, bf16[512,1725]{0,1:T(8,128)(2,1)}, u32[]{:S(2)}) copy-start(bf16[512,1725]{0,1:T(8,128)(2,1)} %param.17) | copy-start | bytes 5299204
  4.4 4.9 %copy-start.7 = (s32[64,64]{1,0:T(8,128)S(1)}, s32[64,64]{1,0:T(8,128)}, u32[]{:S(2)}) copy-start(s32[64,64]{1,0:T(8,128)} %param.11) | copy-start | bytes 49156
  4.4 48.1 %all-to-all-start = ((bf16[4,1,4,4,16,1725]{5,4,2,0,1,3:T(8,128)(2,1)}), bf16[4,1,4,4,16,1725]{5,4,2,0,1,3:T(8,128)(2,1)}, u32[]{:S(2)}, u32[]{:S(2)}) async-start(bf16[4,1,4,4,16,1725]{5,4,2,0,1,3:T(8,128)(2,1)} %copy.71), calls=%async_computation | async-start | bytes 7340032 | tf_op jit(solution)/shard_map/all_to_all | solution.py:61
  52.6 2.6 %copy-start.9 = (bf16[1725,512]{1,0:T(8,128)(2,1)S(1)}, bf16[1725,512]{1,0:T(8,128)(2,1)}, u32[]{:S(2)}) copy-start(bf16[1725,512]{1,0:T(8,128)(2,1)} %param.12) | copy-start | bytes 5299204
  55.0 2.3 copy-start.1
  55.1 3.1 %copy-start.8 = (f32[512]{0:T(512)S(1)}, f32[512]{0:T(512)}, u32[]{:S(2)}) copy-start(f32[512]{0:T(512)} %param.13) | copy-start | bytes 6148
  57.3 1.0 copy-start.3
  59.5 11.8 %collective-permute-start = (bf16[4,4,16,512]{3,2,1,0:T(8,128)(2,1)}, bf16[4,4,16,512]{3,2,1,0:T(8,128)(2,1)S(1)}, u32[]{:S(2)}, u32[]{:S(2)}) collective-permute-start(bf16[4,4,16,512]{3,2,1,0:T(8,128)(2,1)} %get-tuple-element.7), channel_id=1, source_target_pairs={{0,8},{8,16},{16,24},{24,0},{1,9},{9,17},{17,25},{25,1},{2,10},{10... | collective-permute-start | bytes 786440 | tf_op jit(solution)/shard_map/ppermute | solution.py:20
  61.9 13.4 %collective-permute-start.1 = (bf16[4,4,16,512]{3,2,1,0:T(8,128)(2,1)}, bf16[4,4,16,512]{3,2,1,0:T(8,128)(2,1)S(1)}, u32[]{:S(2)}, u32[]{:S(2)}) collective-permute-start(bf16[4,4,16,512]{3,2,1,0:T(8,128)(2,1)} %get-tuple-element.8), channel_id=1, source_target_pairs={{8,0},{16,8},{24,16},{0,24},{9,1},{17,9},{25,17},{1,25},{10,2},{18... | collective-permute-start | bytes 786440 | tf_op jit(solution)/shard_map/ppermute | solution.py:21
  76.5 10.8 %collective-permute-start.2 = (bf16[4,24,4,512]{3,2,1,0:T(4,128)(2,1)}, bf16[4,24,4,512]{3,2,1,0:T(4,128)(2,1)}, u32[]{:S(2)}, u32[]{:S(2)}) collective-permute-start(bf16[4,24,4,512]{3,2,1,0:T(4,128)(2,1)} %get-tuple-element.5), channel_id=1, source_target_pairs={{0,2},{2,4},{4,6},{6,0},{1,3},{3,5},{5,7},{7,1},{8,10},{10,12},{12... | collective-permute-start | bytes 1179656 | tf_op jit(solution)/shard_map/ppermute | solution.py:20
  76.5 10.8 %collective-permute-start.3 = (bf16[4,24,4,512]{3,2,1,0:T(4,128)(2,1)}, bf16[4,24,4,512]{3,2,1,0:T(4,128)(2,1)}, u32[]{:S(2)}, u32[]{:S(2)}) collective-permute-start(bf16[4,24,4,512]{3,2,1,0:T(4,128)(2,1)} %get-tuple-element.6), channel_id=1, source_target_pairs={{2,0},{4,2},{6,4},{0,6},{3,1},{5,3},{7,5},{1,7},{10,8},{12,10},{14... | collective-permute-start | bytes 1179656 | tf_op jit(solution)/shard_map/ppermute | solution.py:21
  84.5 5.7 %copy-start.10 = (bf16[512,1536]{1,0:T(8,128)(2,1)S(1)}, bf16[512,1536]{1,0:T(8,128)(2,1)}, u32[]{:S(2)}) copy-start(bf16[512,1536]{1,0:T(8,128)(2,1)} %param.14) | copy-start | bytes 4718596
  160.5 2.5 %copy-start.4 = (bf16[1024,512]{1,0:T(8,128)(2,1)S(1)}, bf16[1024,512]{1,0:T(8,128)(2,1)}, u32[]{:S(2)}) copy-start(bf16[1024,512]{1,0:T(8,128)(2,1)} %copy-done.3) | copy-start | bytes 3145732
  160.5 2.5 %copy-start.6 = (bf16[512,512]{1,0:T(8,128)(2,1)S(1)}, bf16[512,512]{1,0:T(8,128)(2,1)}, u32[]{:S(2)}) copy-start(bf16[512,512]{1,0:T(8,128)(2,1)} %param.15) | copy-start | bytes 1572868
  162.9 2.0 copy-start.5
  162.9 2.0 copy-start.11
  179.0 4.9 %copy-start.12 = (s32[6]{0:T(128)S(1)}, s32[6]{0:T(128)}, u32[]{:S(2)}) copy-start(s32[6]{0:T(128)} %param.10) | copy-start | bytes 76
  179.0 47.5 %all-to-all-start.1 = ((bf16[4,4,4,1,16,1725]{5,4,2,0,3,1:T(8,128)(2,1)}), bf16[4,4,4,1,16,1725]{5,4,2,0,3,1:T(8,128)(2,1)}, u32[]{:S(2)}, u32[]{:S(2)}) async-start(bf16[4,4,4,1,16,1725]{5,4,2,0,3,1:T(8,128)(2,1)} %copy.84), calls=%async_computation.1 | async-start | bytes 7340032 | tf_op jit(solution)/shard_map/all_to_all | solution.py:103
  226.5 3.1 %copy-start.2 = (bf16[4,4,64,1725]{3,2,1,0:T(8,128)(2,1)S(1)}, bf16[4,4,64,1725]{3,2,1,0:T(8,128)(2,1)}, u32[]{:S(2)}) copy-start(bf16[4,4,64,1725]{3,2,1,0:T(8,128)(2,1)} %param.9) | copy-start | bytes 10598404
where the time goes:
time: 233 us; the launch traced here: 232 us
  waiting for transfers between devices  98.3 us (42%)
  local copies, waits for them, and re-layouts  75.5 us (32%)
  matrix products  28.4 us (12%)
  starting transfers between devices  15.9 us (7%)
  other arithmetic  13.5 us (6%)
    all_to_all x1, waiting for transfers between devices, local(): lax.all_to_all(local_rows, 'lon', split_axis=3, concat_axis=1, tiled=True)  42.5 us
    all_to_all x1, waiting for transfers between devices, local(): lax.all_to_all(outgoing, 'lon', split_axis=1, concat_axis=3, tiled=True)  42.4 us
    reshape x1, local copies, waits for them, and re-layouts, local(): projected.reshape(slots_here, ext_rows // WIN, WIN, ext_cols // WIN, WIN,...  18 us
    transpose x1, local copies, waits for them, and re-layouts, local(): windows.transpose(0, 1, 3, 2, 4, 5, 6, 7)  11.2 us
    ppermute x2, waiting for transfers between devices, with_halo(): before = lax.ppermute(last, axis, up)  9.45 us
    dot_general x1, matrix products, window_mix(): jnp.einsum('bwhqk,bwkhd->bwqhd', weights, windows[:, :, :, 2], preferred_...  9.19 us
    reshape x1, local copies, waits for them, and re-layouts, local(): mixed_heads.reshape(slots_here, ext_rows // WIN, ext_cols // WIN, WIN, WI...  7.36 us
    convert_element_type x1, local copies, waits for them, and re-layouts, window_mix(): return jnp.einsum('bwhqk,bwkhd->bwqhd', weights, windows[:, :, :, 2], pre...  6.99 us
  transfers between devices with their start and end apart: 6, of which 5 were waited for; matrix products, arithmetic and copies ran while one was open for 3% of the time, Pallas kernels for 0%

commit v1 on v0

--- a/solution.py
+++ b/solution.py
@@ -100,7 +100,10 @@
         patches.astype(jnp.float32) + jnp.dot(final_norm, w_dec, preferred_element_type=jnp.float32)
     ).astype(jnp.bfloat16)
     outgoing = predicted.reshape(slots_here, lon_count, rows_here, 1, patch_cols, patch_len)
-    returned = lax.all_to_all(outgoing, "lon", split_axis=1, concat_axis=3, tiled=True)
+    returned = jnp.concatenate(
+        lax.all_to_all(jnp.stack(jnp.split(outgoing, lax.axis_size("lon"), axis=1)), "lon", 0, 0),
+        axis=3,
+    )
     strip_data = returned.reshape(slots_here, rows_here, width_all, patch_len)
     return jnp.where(occupied[:, None, None, None], strip_data, store)
 

time: 233 us -> 233 us (level)
    all_to_all x1 -> x0, local copies, waits for them, and re-layouts: 2.64 us -> none  [local(): lax.all_to_all(outgoing, 'lon', split_axis=1, concat_axis=3, tiled=True)]
    another operation x0 -> x1, local copies, waits for them, and re-layouts: none -> 2.33 us  [local(): jnp.stack(jnp.split(outgoing, lax.axis_size('lon'), axis=1))]
where the time goes in v1:
time: 233 us; the launch traced here: 232 us
  waiting for transfers between devices  98.3 us (42%)
  local copies, waits for them, and re-layouts  73.6 us (32%)
  matrix products  28.4 us (12%)
  starting transfers between devices  16 us (7%)
  other arithmetic  15.6 us (7%)
    all_to_all x1, waiting for transfers between devices, local(): lax.all_to_all(local_rows, 'lon', split_axis=3, concat_axis=1, tiled=True)  42.5 us
    all_to_all x1, waiting for transfers between devices, local(): lax.all_to_all(jnp.stack(jnp.split(outgoing, lax.axis_size('lon'), axis=1...  42.4 us
    reshape x1, local copies, waits for them, and re-layouts, local(): projected.reshape(slots_here, ext_rows // WIN, WIN, ext_cols // WIN, WIN,...  18 us
    transpose x1, local copies, waits for them, and re-layouts, local(): windows.transpose(0, 1, 3, 2, 4, 5, 6, 7)  11.2 us
    ppermute x2, waiting for transfers between devices, with_halo(): before = lax.ppermute(last, axis, up)  9.42 us
    dot_general x1, matrix products, window_mix(): jnp.einsum('bwhqk,bwkhd->bwqhd', weights, windows[:, :, :, 2], preferred_...  9.2 us
    reshape x1, local copies, waits for them, and re-layouts, local(): mixed_heads.reshape(slots_here, ext_rows // WIN, ext_cols // WIN, WIN, WI...  7.36 us
    convert_element_type x1, local copies, waits for them, and re-layouts, window_mix(): return jnp.einsum('bwhqk,bwkhd->bwqhd', weights, windows[:, :, :, 2], pre...  6.98 us
  transfers between devices with their start and end apart: 6, of which 5 were waited for; matrix products, arithmetic and copies ran while one was open for 3% of the time, Pallas kernels for 0%

profile of v1, /device:TPU:0, one launch (start us, length us, event | category | flops | bytes accessed | tf_op | source)
XLA Modules:
  0.0 232.2 jit_solution(5471091866050364807)
XLA Ops:
  0.0 4.4 %copy.84 = bf16[4,1,4,4,16,1725]{5,4,2,0,1,3:T(8,128)(2,1)} copy(bf16[4,1,4,4,16,1725]{5,4,3,2,0,1:T(8,128)(2,1)} %bitcast.66) | data formatting | bytes 7065600 | tf_op jit(solution)/shard_map/reshape | solution.py:60
  4.4 4.9 %all-to-all-start = ((bf16[4,1,4,4,16,1725]{5,4,2,0,1,3:T(8,128)(2,1)}), bf16[4,1,4,4,16,1725]{5,4,2,0,1,3:T(8,128)(2,1)}, u32[]{:S(2)}, u32[]{:S(2)}) async-start(bf16[4,1,4,4,16,1725]{5,4,2,0,1,3:T(8,128)(2,1)} %copy.84), calls=%async_computation | async-start | bytes 7340032 | tf_op jit(solution)/shard_map/all_to_all | solution.py:61
  10.0 42.5 %all-to-all-done = bf16[4,1,4,4,16,1725]{5,4,2,0,1,3:T(8,128)(2,1)} async-done(((bf16[4,1,4,4,16,1725]{5,4,2,0,1,3:T(8,128)(2,1)}), bf16[4,1,4,4,16,1725]{5,4,2,0,1,3:T(8,128)(2,1)}, u32[]{:S(2)}, u32[]{:S(2)}) %all-to-all-start) | async-done | bytes 3532832 | tf_op jit(solution)/shard_map/all_to_all | solution.py:61
  52.6 2.4 %copy.85 = bf16[4,4,1,4,1,16,1725]{6,5,3,1,0,4,2:T(8,128)(2,1)S(1)} copy(bf16[4,4,1,4,1,16,1725]{6,5,3,0,1,4,2:T(8,128)(2,1)} %bitcast.2) | data formatting | bytes 7065600 | tf_op jit(solution)/shard_map/all_to_all | solution.py:61
  55.1 2.1 convert_reduce_fusion
  58.7 0.8 fusion.24
  59.6 2.4 %collective-permute-start = (bf16[4,4,16,512]{3,2,1,0:T(8,128)(2,1)}, bf16[4,4,16,512]{3,2,1,0:T(8,128)(2,1)S(1)}, u32[]{:S(2)}, u32[]{:S(2)}) collective-permute-start(bf16[4,4,16,512]{3,2,1,0:T(8,128)(2,1)} %get-tuple-element.11), channel_id=1, source_target_pairs={{0,8},{8,16},{16,24},{24,0},{1,9},{9,17},{17,25},{25,1},{2,10},{10... | collective-permute-start | bytes 786440 | tf_op jit(solution)/shard_map/ppermute | solution.py:20
  62.0 2.0 collective-permute-start.1
  64.9 6.6 %collective-permute-done = bf16[4,4,16,512]{3,2,1,0:T(8,128)(2,1)S(1)} collective-permute-done((bf16[4,4,16,512]{3,2,1,0:T(8,128)(2,1)}, bf16[4,4,16,512]{3,2,1,0:T(8,128)(2,1)S(1)}, u32[]{:S(2)}, u32[]{:S(2)}) %collective-permute-start) | collective-permute-done | bytes 262176 | tf_op jit(solution)/shard_map/ppermute | solution.py:20
  71.4 4.0 %collective-permute-done.1 = bf16[4,4,16,512]{3,2,1,0:T(8,128)(2,1)S(1)} collective-permute-done((bf16[4,4,16,512]{3,2,1,0:T(8,128)(2,1)}, bf16[4,4,16,512]{3,2,1,0:T(8,128)(2,1)S(1)}, u32[]{:S(2)}, u32[]{:S(2)}) %collective-permute-start.1) | collective-permute-done | bytes 262176 | tf_op jit(solution)/shard_map/ppermute | solution.py:21
  75.4 1.2 pad_maximum_fusion.4
  76.6 1.7 collective-permute-start.3
  78.6 5.9 %copy.86 = bf16[1024,1725]{0,1:T(8,128)(2,1)} copy(bf16[1024,1725]{1,0:T(8,128)(2,1)} %bitcast.64) | data formatting | bytes 7065600 | tf_op jit(solution)/shard_map/reshape | solution.py:62
  84.5 2.9 %collective-permute-done.2 = bf16[4,24,4,512]{3,2,1,0:T(4,128)(2,1)} collective-permute-done((bf16[4,24,4,512]{3,2,1,0:T(4,128)(2,1)}, bf16[4,24,4,512]{3,2,1,0:T(4,128)(2,1)}, u32[]{:S(2)}, u32[]{:S(2)}) %collective-permute-start.2) | collective-permute-done | bytes 393248 | tf_op jit(solution)/shard_map/ppermute | solution.py:20
  87.4 2.8 %pad_maximum_fusion.1 = bf16[4,24,24,512]{3,2,1,0:T(8,128)(2,1)S(1)} fusion(bf16[4,24,4,512]{3,2,1,0:T(4,128)(2,1)} %collective-permute-done.3, bf16[4,4,16,512]{3,2,1,0:T(8,128)(2,1)S(1)} %collective-permute-done.1, bf16[4,16,16,512]{3,2,1,0:T(8,128)(2,1)S(1)} %bitcast.70, bf16[4,4,16,512]{3,2,1,0:T(8,128)(2,1)S(1)} %collective-permute-done, ...), kind=kLoop, calls=%fused_computation.26 | loop fusion | flops 11796480 | bytes 4718592 | tf_op jit(solution)/shard_map/concatenate | solution.py:22
  90.2 5.8 %convolution_convert_fusion = bf16[2304,1536]{1,0:T(8,128)(2,1)} fusion(bf16[2304,512]{1,0:T(8,128)(2,1)S(1)} %bitcast.74, bf16[512,1536]{1,0:T(8,128)(2,1)S(1)} %copy-done.10), kind=kOutput, calls=%fused_computation.3 | convolution fusion | flops 3627417600 | bytes 11010048 | tf_op jit(solution)/shard_map/dot_general | solution.py:67
  96.0 18.0 %reshape.190 = bf16[4,3,8,3,8,3,8,64]{7,6,5,4,3,2,1,0:T(8,128)(2,1)} reshape(bf16[2304,1536]{1,0:T(8,128)(2,1)} %convolution_convert_fusion) | data formatting | bytes 14155776 | tf_op jit(solution)/shard_map/reshape | solution.py:70
  114.0 11.2 %copy.87 = bf16[4,3,3,8,8,3,8,64]{7,4,3,6,2,1,0,5:T(8,128)(2,1)} copy(bf16[4,3,3,8,8,3,8,64]{7,6,5,4,2,3,1,0:T(8,128)(2,1)} %bitcast.62) | data formatting | bytes 14155776 | tf_op jit(solution)/shard_map/transpose | solution.py:73
  125.2 6.4 %fusion.3 = f32[4,9,8,64,64]{3,4,2,1,0:T(8,128)S(1)} fusion(bf16[4,9,64,3,8,64]{5,2,4,1,0,3:T(8,128)(2,1)} %bitcast.60), kind=kOutput, calls=%fused_computation.11 | convolution fusion | flops 150994944 | bytes 14155776 | tf_op jit(solution)/shard_map/bwqhd,bwkhd->bwhqk/dot_general | solution.py:33
  131.6 5.4 %fusion.25 = (f32[4,9,8,64]{3,2,1,0:T(8,128)S(1)}, f32[4,9,8,64,64]{3,4,2,1,0:T(8,128)}) fusion(f32[4,9,8,64,64]{3,4,2,1,0:T(8,128)S(1)} %fusion.3, pred[9,64,64]{1,2,0:T(8,128)(4,1)S(1)} %broadcast_compare_fusion), kind=kOutput, calls=%fused_computation.81 | output fusion | flops 8257599 | bytes 9547776 | tf_op jit(solution)/shard_map/sub | solution.py:42
  137.0 9.2 %convert_bitcast_fusion = bf16[4,9,64,8,64]{2,4,3,1,0:T(8,128)(2,1)} fusion(f32[4,9,8,64,64]{3,4,2,1,0:T(8,128)} %get-tuple-element.16, f32[4,9,8,64]{3,2,1,0:T(8,128)S(1)} %get-tuple-element.15, bf16[4,9,64,3,8,64]{5,2,4,1,0,3:T(8,128)(2,1)} %bitcast.61), kind=kOutput, calls=%fused_computation.14 | convolution fusion | flops 154533888 | bytes 16588800 | tf_op jit(solution)/shard_map/bwhqk,bwkhd->bwqhd/dot_general | solution.py:44
  146.2 7.0 %copy.93 = bf16[4,9,64,8,64]{4,3,2,1,0:T(8,128)(2,1)} copy(bf16[4,9,64,8,64]{2,4,3,1,0:T(8,128)(2,1)} %convert_bitcast_fusion) | data formatting | bytes 4718592 | tf_op jit(solution)/shard_map/convert_element_type | solution.py:46
  153.2 7.4 %reshape.192 = bf16[4,3,3,8,8,512]{5,4,3,2,1,0:T(8,128)(2,1)} reshape(bf16[4,9,64,8,64]{4,3,2,1,0:T(8,128)(2,1)} %copy.93) | data formatting | bytes 4718592 | tf_op jit(solution)/shard_map/reshape | solution.py:90
  160.5 1.9 copy.94
  165.0 4.1 %add_convert_fusion = bf16[1024,1725]{0,1:T(8,128)(2,1)} fusion(bf16[1024,1725]{0,1:T(8,128)(2,1)S(1)} %copy-done.5, bf16[512,1725]{0,1:T(8,128)(2,1)S(1)} %copy-done, f32[1024,512]{1,0:T(8,128)S(1)} %get-tuple-element.18, f32[512]{0:T(512)S(1)} %copy-done.11, f32[1024]{0:T(1024)S(1)} %add_rsqrt_fusion, f32[1024]{0:T(1024)S(1)} %broadcast_multiply_fusion), kind=kOutput, calls=%fused_computation.8 | convolution fusion | flops 1816189952 | bytes 10939392 | tf_op jit(solution)/shard_map/dot_general | solution.py:100
  169.0 5.8 %copy.96 = bf16[1024,1725]{1,0:T(8,128)(2,1)} copy(bf16[1024,1725]{0,1:T(8,128)(2,1)} %add_convert_fusion) | data formatting | bytes 7065600 | tf_op jit(solution)/shard_map/convert_element_type | solution.py:101
  174.8 2.3 %slice_bitcast_fusion.11 = (bf16[1,4,1,4,1,16,1725]{6,5,3,1,4,2,0:T(8,128)(2,1)S(1)}, bf16[1,4,1,4,1,16,1725]{6,5,3,1,4,2,0:T(8,128)(2,1)S(1)}, bf16[1,4,1,4,1,1...) fusion(bf16[4,4,4,1,16,1725]{5,4,2,1,0,3:T(8,128)(2,1)} %bitcast.65), kind=kLoop, calls=%fused_computation.39 | loop fusion | bytes 7065600 | tf_op jit(solution)/shard_map/stack | solution.py:104
  177.1 2.1 pad_maximum_fusion
  179.2 4.9 %all-to-all-start.1 = ((bf16[4,4,1,4,1,16,1725]{6,5,3,1,4,2,0:T(8,128)(2,1)}), bf16[4,4,1,4,1,16,1725]{6,5,3,1,4,2,0:T(8,128)(2,1)}, u32[]{:S(2)}, u32[]{:S(2)}) async-start(bf16[4,4,1,4,1,16,1725]{6,5,3,1,4,2,0:T(8,128)(2,1)} %pad_maximum_fusion), calls=%async_computation.1 | async-start | bytes 7340032 | tf_op jit(solution)/shard_map/all_to_all | solution.py:104
  184.3 42.4 %all-to-all-done.1 = bf16[4,4,1,4,1,16,1725]{6,5,3,1,4,2,0:T(8,128)(2,1)} async-done(((bf16[4,4,1,4,1,16,1725]{6,5,3,1,4,2,0:T(8,128)(2,1)}), bf16[4,4,1,4,1,16,1725]{6,5,3,1,4,2,0:T(8,128)(2,1)}, u32[]{:S(2)}, u32[]{:S(2)}) %all-to-all-start.1) | async-done | bytes 3532832 | tf_op jit(solution)/shard_map/all_to_all | solution.py:104
  226.7 2.6 %copy.100 = bf16[4,1,4,4,1,16,1725]{6,5,3,2,0,4,1:T(8,128)(2,1)S(1)} copy(bf16[4,1,4,4,1,16,1725]{6,5,2,0,4,1,3:T(8,128)(2,1)} %bitcast.24) | data formatting | bytes 7065600 | tf_op jit(solution)/shard_map/reshape | solution.py:103
  229.9 2.3 broadcast_select_fusion
  (55 shorter events, 6.5 us)
Async XLA Ops:
  0.0 164.2 %copy-start = (bf16[512,1725]{0,1:T(8,128)(2,1)S(1)}, bf16[512,1725]{0,1:T(8,128)(2,1)}, u32[]{:S(2)}) copy-start(bf16[512,1725]{0,1:T(8,128)(2,1)} %param.17) | copy-start | bytes 5299204
  4.4 5.0 %copy-start.7 = (s32[64,64]{1,0:T(8,128)S(1)}, s32[64,64]{1,0:T(8,128)}, u32[]{:S(2)}) copy-start(s32[64,64]{1,0:T(8,128)} %param.11) | copy-start | bytes 49156
  4.4 48.1 %all-to-all-start = ((bf16[4,1,4,4,16,1725]{5,4,2,0,1,3:T(8,128)(2,1)}), bf16[4,1,4,4,16,1725]{5,4,2,0,1,3:T(8,128)(2,1)}, u32[]{:S(2)}, u32[]{:S(2)}) async-start(bf16[4,1,4,4,16,1725]{5,4,2,0,1,3:T(8,128)(2,1)} %copy.84), calls=%async_computation | async-start | bytes 7340032 | tf_op jit(solution)/shard_map/all_to_all | solution.py:61
  52.6 2.6 %copy-start.9 = (bf16[1725,512]{1,0:T(8,128)(2,1)S(1)}, bf16[1725,512]{1,0:T(8,128)(2,1)}, u32[]{:S(2)}) copy-start(bf16[1725,512]{1,0:T(8,128)(2,1)} %param.12) | copy-start | bytes 5299204
  55.0 2.3 copy-start.1
  55.1 3.2 %copy-start.8 = (f32[512]{0:T(512)S(1)}, f32[512]{0:T(512)}, u32[]{:S(2)}) copy-start(f32[512]{0:T(512)} %param.13) | copy-start | bytes 6148
  57.3 1.0 copy-start.3
  59.6 11.9 %collective-permute-start = (bf16[4,4,16,512]{3,2,1,0:T(8,128)(2,1)}, bf16[4,4,16,512]{3,2,1,0:T(8,128)(2,1)S(1)}, u32[]{:S(2)}, u32[]{:S(2)}) collective-permute-start(bf16[4,4,16,512]{3,2,1,0:T(8,128)(2,1)} %get-tuple-element.11), channel_id=1, source_target_pairs={{0,8},{8,16},{16,24},{24,0},{1,9},{9,17},{17,25},{25,1},{2,10},{10... | collective-permute-start | bytes 786440 | tf_op jit(solution)/shard_map/ppermute | solution.py:20
  62.0 13.4 %collective-permute-start.1 = (bf16[4,4,16,512]{3,2,1,0:T(8,128)(2,1)}, bf16[4,4,16,512]{3,2,1,0:T(8,128)(2,1)S(1)}, u32[]{:S(2)}, u32[]{:S(2)}) collective-permute-start(bf16[4,4,16,512]{3,2,1,0:T(8,128)(2,1)} %get-tuple-element.12), channel_id=1, source_target_pairs={{8,0},{16,8},{24,16},{0,24},{9,1},{17,9},{25,17},{1,25},{10,2},{18... | collective-permute-start | bytes 786440 | tf_op jit(solution)/shard_map/ppermute | solution.py:21
  76.6 10.8 %collective-permute-start.2 = (bf16[4,24,4,512]{3,2,1,0:T(4,128)(2,1)}, bf16[4,24,4,512]{3,2,1,0:T(4,128)(2,1)}, u32[]{:S(2)}, u32[]{:S(2)}) collective-permute-start(bf16[4,24,4,512]{3,2,1,0:T(4,128)(2,1)} %get-tuple-element.9), channel_id=1, source_target_pairs={{0,2},{2,4},{4,6},{6,0},{1,3},{3,5},{5,7},{7,1},{8,10},{10,12},{12... | collective-permute-start | bytes 1179656 | tf_op jit(solution)/shard_map/ppermute | solution.py:20
  76.6 10.8 %collective-permute-start.3 = (bf16[4,24,4,512]{3,2,1,0:T(4,128)(2,1)}, bf16[4,24,4,512]{3,2,1,0:T(4,128)(2,1)}, u32[]{:S(2)}, u32[]{:S(2)}) collective-permute-start(bf16[4,24,4,512]{3,2,1,0:T(4,128)(2,1)} %get-tuple-element.10), channel_id=1, source_target_pairs={{2,0},{4,2},{6,4},{0,6},{3,1},{5,3},{7,5},{1,7},{10,8},{12,10},{14... | collective-permute-start | bytes 1179656 | tf_op jit(solution)/shard_map/ppermute | solution.py:21
  84.5 5.7 %copy-start.10 = (bf16[512,1536]{1,0:T(8,128)(2,1)S(1)}, bf16[512,1536]{1,0:T(8,128)(2,1)}, u32[]{:S(2)}) copy-start(bf16[512,1536]{1,0:T(8,128)(2,1)} %param.14) | copy-start | bytes 4718596
  160.5 2.5 %copy-start.4 = (bf16[1024,512]{1,0:T(8,128)(2,1)S(1)}, bf16[1024,512]{1,0:T(8,128)(2,1)}, u32[]{:S(2)}) copy-start(bf16[1024,512]{1,0:T(8,128)(2,1)} %copy-done.3) | copy-start | bytes 3145732
  160.5 2.5 %copy-start.6 = (bf16[512,512]{1,0:T(8,128)(2,1)S(1)}, bf16[512,512]{1,0:T(8,128)(2,1)}, u32[]{:S(2)}) copy-start(bf16[512,512]{1,0:T(8,128)(2,1)} %param.15) | copy-start | bytes 1572868
  162.9 2.0 copy-start.5
  163.0 2.0 copy-start.11
  179.2 4.9 %copy-start.12 = (s32[6]{0:T(128)S(1)}, s32[6]{0:T(128)}, u32[]{:S(2)}) copy-start(s32[6]{0:T(128)} %param.10) | copy-start | bytes 76
  179.2 47.5 %all-to-all-start.1 = ((bf16[4,4,1,4,1,16,1725]{6,5,3,1,4,2,0:T(8,128)(2,1)}), bf16[4,4,1,4,1,16,1725]{6,5,3,1,4,2,0:T(8,128)(2,1)}, u32[]{:S(2)}, u32[]{:S(2)}) async-start(bf16[4,4,1,4,1,16,1725]{6,5,3,1,4,2,0:T(8,128)(2,1)} %pad_maximum_fusion), calls=%async_computation.1 | async-start | bytes 7340032 | tf_op jit(solution)/shard_map/all_to_all | solution.py:104
  226.7 3.1 %copy-start.2 = (bf16[4,4,64,1725]{3,2,1,0:T(8,128)(2,1)S(1)}, bf16[4,4,64,1725]{3,2,1,0:T(8,128)(2,1)}, u32[]{:S(2)}) copy-start(bf16[4,4,64,1725]{3,2,1,0:T(8,128)(2,1)} %param.9) | copy-start | bytes 10598404
